TPU v7x, 512 devices: a whole 4x4x16 slice. The times are simulated.
512 devices in a mesh: seq: 128 (over z, y, core), grp: 4 (over x).
Axes of the slice: x: 4, y: 4, z: 16, core: 2. Of those that a mesh axis runs over, the one named last changes fastest.
Arguments:
- tokens: bfloat16 [131072, 512], P('seq'), may hold values from -12 to 12
- w_qkv: bfloat16 [3, 512, 512], P(None, None, 'grp'), may hold values from -0.25 to 0.25
- w_out: bfloat16 [512, 512], replicated, may hold values from -0.75 to 0.75
- w_up: bfloat16 [512, 2048], P(None, 'grp'), may hold values from -0.25 to 0.25
- w_down: bfloat16 [2048, 512], P('grp'), may hold values from -0.125 to 0.125
- score_scale: float32 [8], P('grp'), may hold values from 8 to 400
- patch_list: int32 [128, 3], P('seq'), may hold values from 0 to 127, as said below
- relay_dest: int32 [131072, 1], P('seq'), may hold values from 0 to 127; in each aligned block of 1024 rows (0 to 1023, 1024 to 2047, ...) at most 16 rows name the same one
Outputs:
- relayed: bfloat16 [262144, 512], P('seq', 'grp')
Inputs may be any that keep to these rules, and one draw needn't show every extreme that they name: `patch_list`: row p lists patch p first, then 3 - 1 other distinct patches, each at most 2 patches away from p. `relay_dest`: the rows of one block of 1024 tokens name any one block at most 16 times; in every draw some block names some block exactly 16 times.
All inputs are finite; a program needn't handle non-finite values.
Results may differ from a plain program's by a relative error of at most 0.017.
Values may be sent and summed in bfloat16 or wider, within the bound.
A program may use at most 64 MiB of HBM per device.

v0:
```python
import jax
import jax.numpy as jnp
from jax import lax
from jax.sharding import PartitionSpec as P

PATCH = 1024
REACH = 2
NB = 3


def shifted(block, axis, distance):
    devices = range(lax.axis_size(axis))
    route = [(i - distance, i) for i in devices if i - distance in devices]
    return lax.ppermute(block, axis, route)


def layer_norm(token_rows):
    row_mean = jnp.mean(token_rows, axis=-1, keepdims=True)
    spread = jnp.mean(token_rows * token_rows, axis=-1, keepdims=True) - row_mean * row_mean
    return (token_rows - row_mean) * lax.rsqrt(spread + 1e-05)


def unit_heads(values, head_dim):
    shaped = values.reshape(values.shape[0], -1, head_dim)
    scaled = shaped * lax.rsqrt(jnp.mean(shaped * shaped, axis=-1, keepdims=True) + 1e-06)
    return scaled.reshape(values.shape)


def project(token_rows, weights):
    normed = layer_norm(token_rows.astype(jnp.float32)).astype(jnp.bfloat16)
    return jnp.einsum("nd,cde->cne", normed, weights, preferred_element_type=jnp.float32)


def body(tokens, w_qkv, w_out, w_up, w_down, score_scale, patch_list, relay_dest):
    n_seq = lax.axis_size("seq")
    seq_index = lax.axis_index("seq")
    grp_index = lax.axis_index("grp")
    tok_dev, model_width = tokens.shape
    quarter = w_qkv.shape[2]
    heads_dev = score_scale.shape[0]
    head_dim = quarter // heads_dev
    patch_dev = tok_dev // PATCH
    hop_count = -(-REACH // patch_dev)
    offsets = [offset for offset in range(-hop_count, hop_count + 1) if offset != 0]
    own_products = project(tokens, w_qkv)
    queries = unit_heads(own_products[0], head_dim).astype(jnp.bfloat16)
    key_rows = unit_heads(own_products[1], head_dim).astype(jnp.bfloat16)
    value_rows = own_products[2].astype(jnp.bfloat16)
    fetched_pairs = [shifted((key_rows, value_rows), "seq", -offset) for offset in offsets]
    near_keys = [fetched_pair[0] for fetched_pair in fetched_pairs]
    near_values = [fetched_pair[1] for fetched_pair in fetched_pairs]
    window_keys = jnp.concatenate(near_keys[:hop_count] + [key_rows] + near_keys[hop_count:], 0)
    window_values = jnp.concatenate(
        near_values[:hop_count] + [value_rows] + near_values[hop_count:], 0
    )
    window_count = 2 * hop_count + 1
    key_patches = window_keys.reshape(window_count * patch_dev, PATCH, quarter)
    value_patches = window_values.reshape(window_count * patch_dev, PATCH, quarter)
    first_patch = (seq_index - hop_count) * patch_dev
    relative = patch_list - first_patch
    listed_keys = key_patches[relative].reshape(patch_dev, NB * PATCH, quarter)
    listed_values = value_patches[relative].reshape(patch_dev, NB * PATCH, quarter)
    block_rows = min(512, PATCH)
    block_count = PATCH // block_rows
    query_blocks = queries.reshape(patch_dev, block_count, block_rows, quarter)
    factors = score_scale / head_dim

    def attend(item_index):
        patch_index = item_index // (heads_dev * block_count)
        head_index = item_index // block_count % heads_dev
        block_index = item_index % block_count
        query_block = lax.dynamic_slice_in_dim(
            query_blocks[patch_index, block_index], head_index * head_dim, head_dim, 1
        )
        key_block = lax.dynamic_slice_in_dim(
            listed_keys[patch_index], head_index * head_dim, head_dim, 1
        )
        value_block = lax.dynamic_slice_in_dim(
            listed_values[patch_index], head_index * head_dim, head_dim, 1
        )
        scores = lax.dot_general(
            query_block, key_block, (((1,), (1,)), ((), ())), preferred_element_type=jnp.float32
        )
        scores = scores * factors[head_index]
        row_top = jnp.max(scores, axis=1, keepdims=True)
        exponent = jnp.exp(scores - row_top)
        row_total = jnp.sum(exponent, axis=1, keepdims=True)
        weighted = jnp.dot(
            exponent.astype(jnp.bfloat16), value_block, preferred_element_type=jnp.float32
        )
        return (weighted / row_total).astype(jnp.bfloat16)

    attended = lax.map(attend, jnp.arange(patch_dev * heads_dev * block_count, dtype=jnp.int32))
    attended = attended.reshape(patch_dev, heads_dev, block_count, block_rows, head_dim)
    attended = attended.transpose(0, 2, 3, 1, 4).reshape(tok_dev, quarter)
    head_weights = lax.dynamic_slice_in_dim(w_out, grp_index * quarter, quarter, 0)
    partial_proj = jnp.dot(attended, head_weights, preferred_element_type=jnp.float32)
    proj_share = lax.psum_scatter(
        partial_proj.astype(jnp.bfloat16), "grp", scatter_dimension=1, tiled=True
    ).astype(jnp.float32)
    token_share = lax.dynamic_slice_in_dim(tokens, grp_index * quarter, quarter, 1).astype(
        jnp.float32
    )
    resid = (token_share + proj_share).astype(jnp.bfloat16)
    resid_wide = resid.astype(jnp.float32)
    row_sums = lax.psum(
        (jnp.sum(resid_wide, axis=1), jnp.sum(resid_wide * resid_wide, axis=1)), "grp"
    )
    row_mean = row_sums[0] / model_width
    spread = row_sums[1] / model_width - row_mean * row_mean
    normed_share = ((resid_wide - row_mean[:, None]) * lax.rsqrt(spread + 1e-05)[:, None]).astype(
        jnp.bfloat16
    )
    hidden_pre = jnp.dot(
        lax.all_gather(normed_share, "grp", axis=1, tiled=True),
        w_up,
        preferred_element_type=jnp.float32,
    )
    hidden = jax.nn.gelu(hidden_pre).astype(jnp.bfloat16)
    partial_down = jnp.dot(hidden, w_down, preferred_element_type=jnp.float32)
    down_share = lax.psum_scatter(
        partial_down.astype(jnp.bfloat16), "grp", scatter_dimension=1, tiled=True
    ).astype(jnp.float32)
    out_rows = (resid.astype(jnp.float32) + down_share).astype(jnp.bfloat16)
    capacity = 2 * tok_dev // n_seq
    destination = relay_dest[:, 0]
    onehot = (destination[:, None] == jnp.arange(n_seq, dtype=jnp.int32)[None, :]).astype(jnp.int32)
    before = jnp.cumsum(onehot, axis=0) - onehot
    rank_rows = jnp.sum(before * onehot, axis=1)
    slot_index = destination * capacity + rank_rows
    send_buffer = jnp.zeros((n_seq * capacity, quarter), jnp.bfloat16).at[slot_index].set(out_rows)
    received = lax.all_to_all(
        send_buffer.reshape(n_seq, capacity, quarter),
        "seq",
        split_axis=0,
        concat_axis=0,
        tiled=True,
    )
    return received.reshape(n_seq * capacity, quarter)


def solution(mesh):
    return jax.shard_map(
        body,
        mesh=mesh,
        in_specs=(
            P("seq", None),
            P(None, None, "grp"),
            P(),
            P(None, "grp"),
            P("grp", None),
            P("grp"),
            P("seq", None),
            P("seq", None),
        ),
        out_specs=P("seq", "grp"),
        check_vma=False,
    )
```

profile of v0, /device:TPU:1, one launch (start us, length us, event | category | flops | bytes accessed | tf_op | source)
XLA Modules:
  0.0 281.0 jit_solution(186942135605513350)
XLA Ops:
  9.4 2.0 fusion.36
  13.7 4.7 %collective-permute-start = (bf16[1024,128]{0,1:T(8,128)(2,1)S(1)}, bf16[1024,128]{0,1:T(8,128)(2,1)}, u32[]{:S(2)}, u32[]{:S(2)}) collective-permute-start(bf16[1024,128]{0,1:T(8,128)(2,1)S(1)} %fusion.50), channel_id=1, source_target_pairs={{0,8},{4,12},{8,16},{12,20},{16,24},{20,28},{24,32},{28,36},{32,40... | collective-permute-start | bytes 786440 | tf_op jit(solution)/shard_map/ppermute | solution.py:14
  18.5 3.3 %collective-permute-start.1 = (bf16[1024,128]{0,1:T(8,128)(2,1)S(1)}, bf16[1024,128]{0,1:T(8,128)(2,1)}, u32[]{:S(2)}, u32[]{:S(2)}) collective-permute-start(bf16[1024,128]{0,1:T(8,128)(2,1)S(1)} %fusion.50), channel_id=1, source_target_pairs={{0,4},{4,8},{8,12},{12,16},{16,20},{20,24},{24,28},{28,32},{32,36}... | collective-permute-start | bytes 786440 | tf_op jit(solution)/shard_map/ppermute | solution.py:14
  21.8 4.7 %collective-permute-start.2 = (bf16[1024,128]{0,1:T(8,128)(2,1)S(1)}, bf16[1024,128]{0,1:T(8,128)(2,1)}, u32[]{:S(2)}, u32[]{:S(2)}) collective-permute-start(bf16[1024,128]{0,1:T(8,128)(2,1)S(1)} %fusion.50), channel_id=1, source_target_pairs={{4,0},{8,4},{12,8},{16,12},{20,16},{24,20},{28,24},{32,28},{36,32}... | collective-permute-start | bytes 786440 | tf_op jit(solution)/shard_map/ppermute | solution.py:14
  28.5 4.7 %collective-permute-start.4 = (bf16[1024,128]{0,1:T(8,128)(2,1)}, bf16[1024,128]{0,1:T(8,128)(2,1)}, u32[]{:S(2)}, u32[]{:S(2)}) collective-permute-start(bf16[1024,128]{0,1:T(8,128)(2,1)} %fusion.53), channel_id=1, source_target_pairs={{0,8},{4,12},{8,16},{12,20},{16,24},{20,28},{24,32},{28,36},{32,40... | collective-permute-start | bytes 786440 | tf_op jit(solution)/shard_map/ppermute | solution.py:14
  34.6 1.9 collective-permute-start.5
  37.5 2.4 collective-permute-start.6
  52.9 2.4 copy.26
  56.0 2.0 gather_fusion.1
  58.0 39.8 %while.13 = (s32[]{:T(128)}, bf16[4,512,64]{1,2,0:T(8,128)(2,1)S(1)}, s32[4]{0:T(128)S(1)}, bf16[1,2,512,128]{2,1,3,0:T(2,128)(2,1)S(1)}, bf16[1,3072,128]{2,1,0...) while((s32[]{:T(128)}, ...), condition=%wide.region_10.11_spmd, body=%wide.region_7.10_spmd.sunk | while | flops 415300672 | bytes 20851312 | solution.py:93
  62.2 1.8 multiply_reduce_fusion.2
  65.8 2.2 fusion.79
  75.7 2.2 fusion.79
  82.1 1.8 multiply_reduce_fusion.2
  85.7 2.2 fusion.79
  92.0 1.8 multiply_reduce_fusion.2
  95.6 2.2 fusion.79
  100.1 38.3 %reduce-scatter.7.cloned.1.call-done = bf16[128,1024]{1,0:T(8,128)(2,1)} async-done(((bf16[512,1024]{1,0:T(8,128)(2,1)}), bf16[128,1024]{1,0:T(8,128)(2,1)}) %reduce-scatter.7.cloned.1.call-update) | async-done | bytes 262160
  140.8 7.3 %all-reduce = (f32[1024]{0:T(1024)S(1)}, f32[1024]{0:T(1024)S(1)}) all-reduce(f32[1024]{0:T(1024)S(1)} %get-tuple-element.144, f32[1024]{0:T(1024)S(1)} %get-tuple-element.143), channel_id=1, replica_groups=mesh['seq'=128,'grp'=4] {'grp'}, use_global_device_ids=true, to_apply=%region_15.16 | all-reduce | flops 2048 | bytes 16384 | tf_op jit(solution)/shard_map/psum | solution.py:106
  149.4 35.2 %all-gather.2.cloned.1.call-done = bf16[1024,512]{1,0:T(8,128)(2,1)} async-done(((bf16[1024,128]{1,0:T(8,128)(2,1)}), bf16[1024,512]{1,0:T(8,128)(2,1)}) %all-gather.2.cloned.1.call-update) | async-done | bytes 1048592 | tf_op jit(solution)/shard_map/all_gather | solution.py:115
  184.6 2.7 convolution_convert_fusion.1
  189.6 31.0 %reduce-scatter.9.cloned.1.call-done = bf16[128,1024]{1,0:T(8,128)(2,1)} async-done(((bf16[512,1024]{1,0:T(8,128)(2,1)}), bf16[128,1024]{1,0:T(8,128)(2,1)}) %reduce-scatter.9.cloned.1.call-update) | async-done | bytes 262160
  221.7 3.4 %scatter_custom_fusion = bf16[2048,128]{1,0:T(8,128)(2,1)S(1)} fusion(s32[1024]{0:T(1024)S(1)} %bitcast.114, bf16[1024,128]{1,0:T(8,128)(2,1)S(1)} %get-tuple-element.161, bf16[1024,128]{1,0:T(8,128)(2,1)S(1)} %copy.32, bf16[]{:T(256)} %constant.173.clone.1), kind=kCustom, calls=%fused_computation.67 | custom fusion | flops 524288 | bytes 1048578 | tf_op jit(solution)/shard_map/scatter | solution.py:131
  225.1 48.6 %all_to_all.5 = bf16[128,16,128]{2,1,0:T(8,128)(2,1)S(1)} all-to-all(bf16[128,16,128]{2,1,0:T(8,128)(2,1)S(1)} %bitcast.103), channel_id=1, replica_groups=mesh['seq'=128,'grp'=4] {'seq'}, dimensions={0} | all-to-all | bytes 1048576 | tf_op jit(solution)/shard_map/all_to_all | solution.py:132
  (104 shorter events, 47.8 us)
Async XLA Ops:
  6.5 91.7 %copy-start = (bf16[512,512]{1,0:T(8,128)(2,1)S(1)}, bf16[512,512]{1,0:T(8,128)(2,1)}, u32[]{:S(2)}) copy-start(bf16[512,512]{1,0:T(8,128)(2,1)} %param.12) | copy-start | bytes 1572868
  6.5 131.8 %reduce-scatter.7.cloned.1.call-start = ((), (), s32[]{:S(2)}) async-start(), calls=%async_computation.4 | async-start | bytes 1310720
  11.4 17.2 %copy-start.1 = (f32[1024,384]{0,1}, f32[1024,384]{0,1:S(1)}, u32[]{:S(2)}) copy-start(f32[1024,384]{0,1:S(1)} %fusion.36) | copy-start | bytes 4718596
  13.7 20.6 %copy-start.6 = (f32[2]{0:T(128)S(1)}, f32[2]{0:T(128)}, u32[]{:S(2)}) copy-start(f32[2]{0:T(128)} %param.15) | copy-start | bytes 28
  13.7 20.9 %collective-permute-start = (bf16[1024,128]{0,1:T(8,128)(2,1)S(1)}, bf16[1024,128]{0,1:T(8,128)(2,1)}, u32[]{:S(2)}, u32[]{:S(2)}) collective-permute-start(bf16[1024,128]{0,1:T(8,128)(2,1)S(1)} %fusion.50), channel_id=1, source_target_pairs={{0,8},{4,12},{8,16},{12,20},{16,24},{20,28},{24,32},{28,36},{32,40... | collective-permute-start | bytes 786440 | tf_op jit(solution)/shard_map/ppermute | solution.py:14
  18.5 19.1 %collective-permute-start.1 = (bf16[1024,128]{0,1:T(8,128)(2,1)S(1)}, bf16[1024,128]{0,1:T(8,128)(2,1)}, u32[]{:S(2)}, u32[]{:S(2)}) collective-permute-start(bf16[1024,128]{0,1:T(8,128)(2,1)S(1)} %fusion.50), channel_id=1, source_target_pairs={{0,4},{4,8},{8,12},{12,16},{16,20},{20,24},{24,28},{28,32},{32,36}... | collective-permute-start | bytes 786440 | tf_op jit(solution)/shard_map/ppermute | solution.py:14
  21.8 22.1 %collective-permute-start.2 = (bf16[1024,128]{0,1:T(8,128)(2,1)S(1)}, bf16[1024,128]{0,1:T(8,128)(2,1)}, u32[]{:S(2)}, u32[]{:S(2)}) collective-permute-start(bf16[1024,128]{0,1:T(8,128)(2,1)S(1)} %fusion.50), channel_id=1, source_target_pairs={{4,0},{8,4},{12,8},{16,12},{20,16},{24,20},{28,24},{32,28},{36,32}... | collective-permute-start | bytes 786440 | tf_op jit(solution)/shard_map/ppermute | solution.py:14
  26.5 18.4 %collective-permute-start.3 = (bf16[1024,128]{0,1:T(8,128)(2,1)S(1)}, bf16[1024,128]{0,1:T(8,128)(2,1)}, u32[]{:S(2)}, u32[]{:S(2)}) collective-permute-start(bf16[1024,128]{0,1:T(8,128)(2,1)S(1)} %fusion.50), channel_id=1, source_target_pairs={{8,0},{12,4},{16,8},{20,12},{24,16},{28,20},{32,24},{36,28},{40,32... | collective-permute-start | bytes 786440 | tf_op jit(solution)/shard_map/ppermute | solution.py:14
  28.5 12.4 %collective-permute-start.4 = (bf16[1024,128]{0,1:T(8,128)(2,1)}, bf16[1024,128]{0,1:T(8,128)(2,1)}, u32[]{:S(2)}, u32[]{:S(2)}) collective-permute-start(bf16[1024,128]{0,1:T(8,128)(2,1)} %fusion.53), channel_id=1, source_target_pairs={{0,8},{4,12},{8,16},{12,20},{16,24},{20,28},{24,32},{28,36},{32,40... | collective-permute-start | bytes 786440 | tf_op jit(solution)/shard_map/ppermute | solution.py:14
  33.3 1.3 copy-start.7
  34.6 11.3 %collective-permute-start.5 = (bf16[1024,128]{0,1:T(8,128)(2,1)}, bf16[1024,128]{0,1:T(8,128)(2,1)S(1)}, u32[]{:S(2)}, u32[]{:S(2)}) collective-permute-start(bf16[1024,128]{0,1:T(8,128)(2,1)} %fusion.53), channel_id=1, source_target_pairs={{0,4},{4,8},{8,12},{12,16},{16,20},{20,24},{24,28},{28,32},{32,36}... | collective-permute-start | bytes 786440 | tf_op jit(solution)/shard_map/ppermute | solution.py:14
  37.5 13.7 %collective-permute-start.6 = (bf16[1024,128]{0,1:T(8,128)(2,1)}, bf16[1024,128]{0,1:T(8,128)(2,1)S(1)}, u32[]{:S(2)}, u32[]{:S(2)}) collective-permute-start(bf16[1024,128]{0,1:T(8,128)(2,1)} %fusion.53), channel_id=1, source_target_pairs={{4,0},{8,4},{12,8},{16,12},{20,16},{24,20},{28,24},{32,28},{36,32}... | collective-permute-start | bytes 786440 | tf_op jit(solution)/shard_map/ppermute | solution.py:14
  41.0 11.1 %collective-permute-start.7 = (bf16[1024,128]{0,1:T(8,128)(2,1)}, bf16[1024,128]{0,1:T(8,128)(2,1)S(1)}, u32[]{:S(2)}, u32[]{:S(2)}) collective-permute-start(bf16[1024,128]{0,1:T(8,128)(2,1)} %fusion.53), channel_id=1, source_target_pairs={{8,0},{12,4},{16,8},{20,12},{24,16},{28,20},{32,24},{36,28},{40,32... | collective-permute-start | bytes 786440 | tf_op jit(solution)/shard_map/ppermute | solution.py:14
  45.9 1.1 copy-start.2
  100.0 84.6 %copy-start.4 = (bf16[512,512]{1,0:T(8,128)(2,1)S(1)}, bf16[512,512]{1,0:T(8,128)(2,1)}, u32[]{:S(2)}) copy-start(bf16[512,512]{1,0:T(8,128)(2,1)} %param.14) | copy-start | bytes 1572868
  100.0 84.6 %copy-start.5 = (bf16[512,512]{1,0:T(8,128)(2,1)S(1)}, bf16[512,512]{1,0:T(8,128)(2,1)}, u32[]{:S(2)}) copy-start(bf16[512,512]{1,0:T(8,128)(2,1)} %param.13) | copy-start | bytes 1572868
  100.0 84.6 %all-gather.2.cloned.1.call-start = ((), (), s32[]{:S(2)}) async-start(), calls=%async_computation.3 | async-start | bytes 1310720 | tf_op jit(solution)/shard_map/all_gather | solution.py:115
  149.2 71.4 %reduce-scatter.9.cloned.1.call-start = ((), (), s32[]{:S(2)}) async-start(), calls=%async_computation.5 | async-start | bytes 1310720
  187.3 1.4 copy-start.3
Sparse Core Ops, SparseCore 0:
  100.1 38.1 reduce-scatter.6
  149.3 35.2 all-gather.1
  188.8 31.7 reduce-scatter.8
where the time goes:
time: 284 us; the launch traced here: 281 us
  waiting for transfers between devices  105 us (37%)
  blocking collectives  56 us (20%)
  local copies, waits for them, and re-layouts  32.6 us (11%)
  starting transfers between devices  24.6 us (9%)
  matrix products  21.2 us (7%)
  other arithmetic  17.8 us (6%)
  between operations  13.6 us (5%)
  loops' own time  10.7 us (4%)
    unnamed x5, waiting for transfers between devices  69.3 us
    all_to_all x1, blocking collectives, body(): lax.all_to_all(send_buffer.reshape(n_seq, capacity, quarter), 'seq', spli...  48.6 us
    all_gather x1, waiting for transfers between devices, body(): lax.all_gather(normed_share, 'grp', axis=1, tiled=True)  35.2 us
    ppermute x8, starting transfers between devices, shifted(): return lax.ppermute(block, axis, route)  24.4 us
    unnamed x31, local copies, waits for them, and re-layouts  15.9 us
    another operation x1, loops' own time, body(): lax.map(attend, jnp.arange(patch_dev * heads_dev * block_count, dtype=jnp...  10.7 us
    dot_general x4, matrix products, attend(): jnp.dot(exponent.astype(jnp.bfloat16), value_block, preferred_element_typ...  8.91 us
    psum x1, blocking collectives, body(): lax.psum((jnp.sum(resid_wide, axis=1), jnp.sum(resid_wide * resid_wide, a...  7.34 us
  transfers between devices with their start and end apart: 11, of which 3 were waited for; matrix products, arithmetic and copies ran while one was open for 5% of the time, Pallas kernels for 0%

commit v1 on v0

v1 whole, which is shorter than its diff:
```python
import functools

import jax
import jax.numpy as jnp
from jax import lax
from jax.experimental import pallas as pl
from jax.experimental.pallas import tpu as pltpu
from jax.sharding import PartitionSpec as P

MESH = pl.DeviceIdType.MESH
F32 = jnp.float32
BF16 = jnp.bfloat16
PATCH = 1024
LOG2E = 1.4426950408889634
OFFSETS = (1, -1, 2, -2)


def layer_norm(rows):
    mean = jnp.mean(rows, axis=-1, keepdims=True)
    spread = jnp.mean(rows * rows, axis=-1, keepdims=True) - mean * mean
    return (rows - mean) * lax.rsqrt(spread + 1e-05)


def unit_heads(rows, low):
    squares = rows * rows
    first = jnp.sum(jnp.where(low, squares, 0.0), axis=-1, keepdims=True)
    second = jnp.sum(jnp.where(low, 0.0, squares), axis=-1, keepdims=True)
    factor = jnp.where(
        low, lax.rsqrt(first / 64.0 + 1e-06), lax.rsqrt(second / 64.0 + 1e-06)
    )
    return rows * factor


def gelu(rows):
    return 0.5 * rows * (1.0 + jnp.tanh(0.7978845608028654 * (rows + 0.044715 * rows * rows * rows)))


def kernel(
    n_seq, n_grp, tokens, w_qkv, w_out, w_up, w_down, scale, patches, dest_ref, out,
    queries, kv_first, kv_second, acc, tops, part, att, up_x, down_x, rows_full, rows, place, send_rows,
    halo_send, halo_recv, w_send, w_recv, f_send, f_recv, a_send, a_recv, b_send, b_recv,
    relay_send, relay_recv, local_sem, late_sem,
):
    s = lax.axis_index("seq")
    g = lax.axis_index("grp")
    depth = n_seq // 8
    z = s // 8
    yc = s % 8
    core = s % 2

    def near(offset):
        return (s + offset + n_seq) % n_seq

    kv = (kv_first, kv_second)
    barrier = pltpu.get_barrier_semaphore()

    def greet(sem, seq, grp):
        pl.semaphore_signal(sem, inc=1, device_id=(seq, grp), device_id_type=MESH)

    for k in range(1, n_grp):
        greet(barrier, s, (g + k) % n_grp)
    for offset in OFFSETS:
        greet(barrier, near(offset), g)
    for k in range(1, 8):
        greet(barrier, z * 8 + (yc + k) % 8, g)
    for k in range(1, depth):
        greet(barrier, ((z + k) % depth) * 8 + yc, g)

    pl.semaphore_wait(barrier, n_grp - 1 + len(OFFSETS) + 7 + depth - 1)

    half = pl.ds(pl.multiple_of(core * 256, 256), 256)

    def weight_copy(which, hop):
        src = (w_up, w_down)[which]
        dst = (up_x, down_x)[which]
        return pltpu.make_async_remote_copy(
            src_ref=src.at[half],
            dst_ref=dst.at[hop - 1, half],
            send_sem=w_send.at[which, hop - 1],
            recv_sem=w_recv.at[which, hop - 1],
            device_id=(s, (g + n_grp - hop) % n_grp),
            device_id_type=MESH,
        )

    def forward_copy(which, hop):
        buf = (up_x, down_x)[which]
        return pltpu.make_async_remote_copy(
            src_ref=buf.at[hop - 1, half],
            dst_ref=buf.at[hop - 1, half],
            send_sem=f_send.at[which, hop - 1],
            recv_sem=f_recv.at[which, hop - 1],
            device_id=(s + 1 - 2 * core, g),
            device_id_type=MESH,
        )

    for which in range(2):
        for hop in (1, 3, 2):
            weight_copy(which, hop).start()

    for k in range(1, 8):
        greet(late_sem, z * 8 + (yc + k) % 8, g)

    low = lax.broadcasted_iota(jnp.int32, (1, 128), 1) < 64

    def project(block, _):
        at = pl.ds(pl.multiple_of(block * 256, 256), 256)
        normed = layer_norm(tokens[at, :].astype(F32)).astype(BF16)
        q = unit_heads(jnp.dot(normed, w_qkv[0], preferred_element_type=F32), low)
        k = unit_heads(jnp.dot(normed, w_qkv[1], preferred_element_type=F32), low)
        v = jnp.dot(normed, w_qkv[2], preferred_element_type=F32)
        queries[0, at, :] = jnp.where(low, q, 0.0).astype(BF16)
        queries[1, at, :] = jnp.where(low, pltpu.roll(q, 64, 1), 0.0).astype(BF16)
        kv_first[2, at, :] = jnp.where(low, k, pltpu.roll(v, 64, 1)).astype(BF16)
        kv_second[2, at, :] = jnp.where(low, pltpu.roll(k, 64, 1), v).astype(BF16)
        return 0

    lax.fori_loop(0, 4, project, 0)

    def halo_copy(head, index):
        offset = OFFSETS[index]
        return pltpu.make_async_remote_copy(
            src_ref=kv[head].at[2],
            dst_ref=kv[head].at[2 - offset],
            send_sem=halo_send.at[head, index],
            recv_sem=halo_recv.at[head, index],
            device_id=(near(offset), g),
            device_id_type=MESH,
        )

    for head in range(2):
        for index in range(4):
            halo_copy(head, index).start()

    def scores_of(head, at, rel):
        return lax.dot_general(
            queries[head, at, :], kv[head][rel], (((1,), (1,)), ((), ())), preferred_element_type=F32
        )

    def weighted(head, exponent, rel):
        values = jnp.where(low, jnp.asarray(1.0, BF16), kv[head][rel])
        return jnp.dot(exponent.astype(BF16), values, preferred_element_type=F32)

    factors = [scale[head] * (LOG2E / 64.0) for head in range(2)]

    def own_patch(head):
        def step(block, _):
            at = pl.ds(pl.multiple_of(block * 256, 256), 256)
            scores = scores_of(head, at, 2)
            top = jnp.max(scores, axis=1, keepdims=True)
            acc[head, at, :] = weighted(head, jnp.exp2((scores - top) * factors[head]), 2)
            tops[head, at, :] = top
            return 0

        lax.fori_loop(0, 4, step, 0)

    for head in range(2):
        own_patch(head)

    dest = dest_ref[...]
    dz = (dest // 8 - z + depth) % depth
    lag = jnp.minimum(dz, depth - dz)
    order = jnp.where(dz * 2 == depth, 0, jnp.where(dz == 0, depth - 1, 2 * (depth // 2 - lag) - jnp.where(dz * 2 < depth, 0, 1)))
    position = order * 8 + (dest % 8 - yc + 8) % 8
    onehot = (lax.broadcasted_iota(jnp.int32, (n_seq, PATCH), 0) == position).astype(F32)
    earlier = (
        lax.broadcasted_iota(jnp.int32, (PATCH, PATCH), 0)
        < lax.broadcasted_iota(jnp.int32, (PATCH, PATCH), 1)
    ).astype(F32).astype(BF16)
    before = jnp.dot(onehot.astype(BF16), earlier, preferred_element_type=F32)
    rank = jnp.sum(before * onehot, axis=0, keepdims=True).astype(jnp.int32)
    slot = position * 16 + rank

    def place_rows(block, _):
        at = pl.ds(pl.multiple_of(block * 256, 256), 256)
        index = lax.broadcasted_iota(jnp.int32, (256, PATCH), 0) + block * 256
        place[at, :] = (index == slot).astype(F32).astype(BF16)
        return 0

    lax.fori_loop(0, n_seq * 16 // 256, place_rows, 0)

    for hop in (1, 3, 2):
        weight_copy(0, hop).wait_recv()
        forward_copy(0, hop).start()

    rels = [jnp.clip(patches[0, i] - s + 2, 0, 4) for i in (1, 2)]

    def rest(head, at):
        pair = [scores_of(head, at, rel) for rel in rels]
        top = jnp.maximum(
            jnp.max(pair[0], axis=1, keepdims=True), jnp.max(pair[1], axis=1, keepdims=True)
        )
        own_top = tops[head, at, :]
        top = jnp.maximum(top, own_top)
        total = acc[head, at, :] * jnp.exp2((own_top - top) * factors[head])
        for rel, scores in zip(rels, pair):
            total = total + weighted(head, jnp.exp2((scores - top) * factors[head]), rel)
        return total

    for index in range(4):
        halo_copy(0, index).wait_recv()

    def first_head(block, _):
        at = pl.ds(pl.multiple_of(block * 256, 256), 256)
        acc[0, at, :] = rest(0, at)
        return 0

    lax.fori_loop(0, 4, first_head, 0)

    for hop in (1, 3, 2):
        weight_copy(1, hop).wait_recv()
        forward_copy(1, hop).start()

    for index in range(4):
        halo_copy(1, index).wait_recv()

    quarter = pl.ds(pl.multiple_of(g * 128, 128), 128)

    def att_copy(turn):
        block = (g + 1 + turn) % n_grp
        at = pl.ds(pl.multiple_of(block * 256, 256), 256)
        return pltpu.make_async_remote_copy(
            src_ref=part.at[at],
            dst_ref=att.at[:, quarter],
            send_sem=a_send.at[turn],
            recv_sem=a_recv.at[turn],
            device_id=(s, block),
            device_id_type=MESH,
        )

    def finish(block):
        at = pl.ds(pl.multiple_of(block * 256, 256), 256)
        second = rest(1, at)
        first = acc[0, at, :]
        numer = jnp.where(low, pltpu.roll(first, 64, 1), second)
        denom = jnp.where(low, first, pltpu.roll(second, 64, 1))
        return (numer / denom).astype(BF16)

    def second_head(turn, _):
        block = (g + 1 + turn) % n_grp
        at = pl.ds(pl.multiple_of(block * 256, 256), 256)
        part[at, :] = finish(block)
        att_copy(turn).start()
        return 0

    lax.fori_loop(0, 3, second_head, 0)
    att[:, quarter] = finish(g)

    mine = pl.ds(pl.multiple_of(g * 256, 256), 256)
    for turn in range(3):
        att_copy(turn).wait_recv()
    resid = (
        tokens[mine, :].astype(F32)
        + jnp.dot(att[...], w_out[...], preferred_element_type=F32)
    ).astype(BF16)
    resid_wide = resid.astype(F32)
    normed = layer_norm(resid_wide).astype(BF16)

    def mlp(up, down):
        hidden = gelu(jnp.dot(normed, up, preferred_element_type=F32)).astype(BF16)
        product = jnp.dot(hidden, down, preferred_element_type=F32)
        return product.astype(BF16).astype(F32)

    total = mlp(w_up[...], w_down[...])
    for hop in (1, 3, 2):
        forward_copy(0, hop).wait_recv()
        forward_copy(1, hop).wait_recv()
        total = total + mlp(up_x[hop - 1], down_x[hop - 1])
    rows_full[...] = (resid_wide + total).astype(BF16)

    def back_copy(hop):
        target = (g + hop) % n_grp
        return pltpu.make_async_remote_copy(
            src_ref=rows_full.at[:, pl.ds(pl.multiple_of(target * 128, 128), 128)],
            dst_ref=rows.at[mine],
            send_sem=b_send.at[hop - 1],
            recv_sem=b_recv.at[hop - 1],
            device_id=(s, target),
            device_id_type=MESH,
        )

    for hop in (1, 3, 2):
        back_copy(hop).start()
    rows[mine, :] = rows_full[:, quarter]
    for hop in (1, 3, 2):
        back_copy(hop).wait_recv()

    pl.semaphore_wait(late_sem, 7)

    def relay_copy(k):
        m = k // 8
        h = (m + 1) // 2
        dz = jnp.where(m % 2 == 1, depth // 2 + h, depth // 2 - h) % depth
        target = ((z + dz) % depth) * 8 + (yc + k % 8) % 8
        return pltpu.make_async_remote_copy(
            src_ref=send_rows.at[pl.ds(pl.multiple_of(k * 16, 16), 16)],
            dst_ref=out.at[pl.ds(pl.multiple_of(s * 16, 16), 16)],
            send_sem=relay_send,
            recv_sem=relay_recv,
            device_id=(target, g),
            device_id_type=MESH,
        )

    def spread(chunk):
        at = pl.ds(pl.multiple_of(chunk * 256, 256), 256)
        send_rows[at, :] = jnp.dot(place[at, :], rows[...], preferred_element_type=F32).astype(BF16)

    def relay(k, _):
        relay_copy(k).start()
        return 0

    def relay_chunk(chunk, _):
        spread(chunk)
        lax.fori_loop(chunk * 16, chunk * 16 + 16, relay, 0)
        return 0

    last = n_seq // 16 - 1
    self_k = n_seq - 8
    lax.fori_loop(0, last, relay_chunk, 0)
    spread(last)
    lax.fori_loop(last * 16, self_k, relay, 0)
    lax.fori_loop(self_k + 1, n_seq, relay, 0)
    own = pltpu.make_async_copy(
        send_rows.at[pl.ds(self_k * 16, 16)],
        out.at[pl.ds(pl.multiple_of(s * 16, 16), 16)],
        local_sem,
    )
    own.start()
    own.wait()

    for which in range(2):
        for hop in (1, 2, 3):
            weight_copy(which, hop).wait_send()
            forward_copy(which, hop).wait_send()
    for head in range(2):
        for index in range(4):
            halo_copy(head, index).wait_send()
    for turn in range(3):
        att_copy(turn).wait_send()
        back_copy(turn + 1).wait_send()
    sent = pl.ds(0, (n_seq - 1) * 16)
    pltpu.make_async_copy(send_rows.at[sent], send_rows.at[sent], relay_send).wait()
    pltpu.make_async_copy(send_rows.at[sent], out.at[sent], relay_recv).wait()


def solution(mesh):
    n_seq = mesh.shape["seq"]
    n_grp = mesh.shape["grp"]

    def body(tokens, w_qkv, w_out, w_up, w_down, score_scale, patch_list, relay_dest):
        vmem = pl.BlockSpec(memory_space=pltpu.VMEM)
        smem = pl.BlockSpec(memory_space=pltpu.SMEM)
        dma = pltpu.SemaphoreType.DMA
        return pl.pallas_call(
            functools.partial(kernel, n_seq, n_grp),
            out_shape=jax.ShapeDtypeStruct((n_seq * 16, 128), BF16),
            in_specs=[vmem] * 5 + [smem, smem, vmem],
            out_specs=vmem,
            scratch_shapes=[
                pltpu.VMEM((2, PATCH, 128), BF16),
                pltpu.VMEM((5, PATCH, 128), BF16),
                pltpu.VMEM((5, PATCH, 128), BF16),
                pltpu.VMEM((2, PATCH, 128), F32),
                pltpu.VMEM((2, PATCH, 1), F32),
                pltpu.VMEM((PATCH, 128), BF16),
                pltpu.VMEM((256, 512), BF16),
                pltpu.VMEM((3, 512, 512), BF16),
                pltpu.VMEM((3, 512, 512), BF16),
                pltpu.VMEM((256, 512), BF16),
                pltpu.VMEM((PATCH, 128), BF16),
                pltpu.VMEM((n_seq * 16, PATCH), BF16),
                pltpu.VMEM((n_seq * 16, 128), BF16),
                dma((2, 4)),
                dma((2, 4)),
                dma((2, 3)),
                dma((2, 3)),
                dma((2, 3)),
                dma((2, 3)),
                dma((3,)),
                dma((3,)),
                dma((3,)),
                dma((3,)),
                dma,
                dma,
                dma,
                pltpu.SemaphoreType.REGULAR,
            ],
            compiler_params=pltpu.CompilerParams(
                collective_id=0, has_side_effects=True, vmem_limit_bytes=56 << 20
            ),
            name="block",
        )(tokens, w_qkv, w_out, w_up, w_down, score_scale, patch_list, relay_dest.reshape(1, PATCH))

    return jax.shard_map(
        body,
        mesh=mesh,
        in_specs=(
            P("seq", None),
            P(None, None, "grp"),
            P(),
            P(None, "grp"),
            P("grp", None),
            P("grp"),
            P("seq", None),
            P("seq", None),
        ),
        out_specs=P("seq", "grp"),
        check_vma=False,
    )
```

time: 284 us -> 86.5 us (0.30)
  waiting for transfers between devices: 105 us -> 0 us
  Pallas kernels: 0 us -> 84.4 us
  blocking collectives: 56 us -> 0 us
  local copies, waits for them, and re-layouts: 32.6 us -> 1.87 us
  starting transfers between devices: 24.6 us -> 0 us
  matrix products: 21.2 us -> 0 us
  other arithmetic: 17.8 us -> 0 us
  between operations: 13.6 us -> 0.01 us
  loops' own time: 10.7 us -> 0 us
    pallas_call x0 -> x1, Pallas kernels: none -> 84.4 us  [body(): pl.pallas_call(functools.partial(kernel, n_seq, n_grp), out_shape=jax.Sha...]
    unnamed x5 -> x0, waiting for transfers between devices: 69.3 us -> none
    all_to_all x1 -> x0, blocking collectives: 48.6 us -> none  [body(): lax.all_to_all(send_buffer.reshape(n_seq, capacity, quarter), 'seq', spli...]
    all_gather x1 -> x0, waiting for transfers between devices: 35.2 us -> none  [body(): lax.all_gather(normed_share, 'grp', axis=1, tiled=True)]
    ppermute x8 -> x0, starting transfers between devices: 24.4 us -> none  [shifted(): return lax.ppermute(block, axis, route)]
    dot_general x10 -> x0, matrix products: 19.2 us -> none  [the longest x4 8.91 us: attend(): jnp.dot(exponent.astype(jnp.bfloat16), value_block, preferred_element_typ...]
    unnamed x31 -> x1, local copies, waits for them, and re-layouts: 15.9 us -> 1.87 us
    reduce_sum x9 -> x0, other arithmetic: 11.6 us -> none  [the longest x4 7.18 us: attend(): row_total = jnp.sum(exponent, axis=1, keepdims=True)]
  transfers between devices with their start and end apart: 11 -> 0, of which waited for: 3 -> 0; matrix products, arithmetic and copies ran while one was open for 5% -> 0% of each run, Pallas kernels for 0% -> 0%
where the time goes in v1:
time: 86.5 us; the launch traced here: 86.3 us
  Pallas kernels  84.4 us (98%)
  local copies, waits for them, and re-layouts  1.87 us (2%)
    pallas_call x1, Pallas kernels, body(): pl.pallas_call(functools.partial(kernel, n_seq, n_grp), out_shape=jax.Sha...  84.4 us
    unnamed x1, local copies, waits for them, and re-layouts  1.87 us

profile of v1, /device:TPU:1, one launch (start us, length us, event | category | flops | bytes accessed | tf_op | source)
XLA Modules:
  0.0 86.3 jit_solution(11097763768077737450)
XLA Ops:
  0.0 84.4 %block.1 = bf16[2048,128]{1,0:T(8,128)(2,1)} custom-call(bf16[1024,512]{1,0:T(8,128)(2,1)} %tokens.1, bf16[3,512,128]{2,1,0:T(8,128)(2,1)} %w_qkv.1, bf16[512,512]{1,0:T(8,128)(2,1)} %w_out.1, bf16[512,512]{1,0:T(8,128)(2,1)} %w_up.1, bf16[512,512]{1,0:T(8,128)(2,1)} %w_down.1, f32[2]{0:T(128)} %scale.1, s32[1,3]{1,0:T(1,128)} %patches.1, s32[1,1024]{1,0:T(1,128)} %bitcast.1), custom_call_target="tpu_custom_call" | custom-call | tf_op jit(solution)/shard_map/block/pallas_call | solution.py:353
  84.4 1.9 %copy.10 = bf16[2048,128]{1,0:T(8,128)(2,1)} copy(bf16[2048,128]{1,0:T(8,128)(2,1)} %block.1) | data formatting | bytes 1048576

commit v2 on v1

v2 whole, which is shorter than its diff:
```python
import functools

import jax
import jax.numpy as jnp
from jax import lax
from jax.experimental import pallas as pl
from jax.experimental.pallas import tpu as pltpu
from jax.sharding import PartitionSpec as P

MESH = pl.DeviceIdType.MESH
F32 = jnp.float32
BF16 = jnp.bfloat16
PATCH = 1024
LOG2E = 1.4426950408889634


def layer_norm(rows):
    mean = jnp.mean(rows, axis=-1, keepdims=True)
    spread = jnp.mean(rows * rows, axis=-1, keepdims=True) - mean * mean
    return (rows - mean) * lax.rsqrt(spread + 1e-05)


def unit_heads(rows, low):
    squares = rows * rows
    first = jnp.sum(jnp.where(low, squares, 0.0), axis=-1, keepdims=True)
    second = jnp.sum(jnp.where(low, 0.0, squares), axis=-1, keepdims=True)
    factor = jnp.where(
        low, lax.rsqrt(first / 64.0 + 1e-06), lax.rsqrt(second / 64.0 + 1e-06)
    )
    return rows * factor


def unit_head_columns(columns):
    return columns * lax.rsqrt(jnp.mean(columns * columns, axis=0, keepdims=True) + 1e-06)


def gelu(rows):
    return 0.5 * rows * (1.0 + jnp.tanh(0.7978845608028654 * (rows + 0.044715 * rows * rows * rows)))


def kernel(
    n_seq, n_grp, tokens_in, qkv_in, out_in, up_in, down_in, scale, patches, dest_ref, out,
    tokens, w_qkv, w_out, up, down, queries, kv_0, kv_1, kv_2, kv_3, acc, tops, part, att,
    rows_full, rows, place, send_rows,
    load_sem, halo_send, halo_recv, w_send, w_recv, t_send, t_recv, f_send, f_recv,
    a_send, a_recv, b_send, b_recv, relay_send, relay_recv, local_sem, late_sem,
):
    s = lax.axis_index("seq")
    g = lax.axis_index("grp")
    depth = n_seq // 8
    z = s // 8
    yc = s % 8
    core = s % 2
    sibling = s + 1 - 2 * core
    kv = (kv_0, kv_1, kv_2, kv_3)

    def block_of(index, size=256):
        return pl.ds(pl.multiple_of(index * size, size), size)

    token_loads = [
        pltpu.make_async_copy(
            tokens_in.at[pl.ds(256 * b, 256)], tokens.at[pl.ds(256 * b, 256)], load_sem.at[b]
        )
        for b in range(4)
    ]
    qkv_load = pltpu.make_async_copy(qkv_in, w_qkv, load_sem.at[4])
    out_load = pltpu.make_async_copy(out_in, w_out, load_sem.at[5])
    up_load = pltpu.make_async_copy(up_in, up.at[0], load_sem.at[6])
    down_load = pltpu.make_async_copy(down_in, down.at[0], load_sem.at[7])
    token_loads[0].start()
    qkv_load.start()
    for b in range(1, 4):
        token_loads[b].start()
    up_load.start()
    down_load.start()
    out_load.start()

    barrier = pltpu.get_barrier_semaphore()

    def greet(sem, seq, grp):
        pl.semaphore_signal(sem, inc=1, device_id=(seq, grp), device_id_type=MESH)

    for k in range(1, n_grp):
        greet(barrier, s, (g + k) % n_grp)
    for offset in (2, -2):
        greet(barrier, (s + offset + n_seq) % n_seq, g)
    for k in range(1, 8):
        greet(barrier, z * 8 + (yc + k) % 8, g)
    for k in range(1, depth):
        greet(barrier, ((z + k) % depth) * 8 + yc, g)

    low = lax.broadcasted_iota(jnp.int32, (1, 128), 1) < 64

    def project(block):
        at = pl.ds(256 * block, 256)
        token_loads[block].wait()
        if block == 0:
            qkv_load.wait()
        normed = layer_norm(tokens[at, :].astype(F32)).astype(BF16)
        q = jnp.dot(normed, w_qkv[0], preferred_element_type=F32).T
        k = unit_heads(jnp.dot(normed, w_qkv[1], preferred_element_type=F32), low)
        v = jnp.dot(normed, w_qkv[2], preferred_element_type=F32).T.astype(BF16)
        for head in range(2):
            mine = pl.ds(64 * head, 64)
            queries[head, mine, at] = unit_head_columns(q[64 * head : 64 * head + 64]).astype(BF16)
            queries[head, pl.ds(64 - 64 * head, 64), at] = jnp.zeros((64, 256), BF16)
        kv[block][2, 0] = k.astype(BF16)
        kv[block][2, 1, pl.ds(0, 128)] = v[:, :128]
        kv[block][2, 1, pl.ds(128, 128)] = v[:, 128:]

    def halo_copy(chunk, index):
        target = ((s + 2) % n_seq, (s - 2 + n_seq) % n_seq, sibling, sibling)[index]
        src = (2, 2, 2, 4 - 4 * core)[index]
        dst = (0, 4, 1 + 2 * core, 3 - 2 * core)[index]
        return pltpu.make_async_remote_copy(
            src_ref=kv[chunk].at[src],
            dst_ref=kv[chunk].at[dst],
            send_sem=halo_send.at[chunk, index],
            recv_sem=halo_recv.at[chunk, index],
            device_id=(target, g),
            device_id_type=MESH,
        )

    half = block_of(core)
    part_rows = [pl.ds(pl.multiple_of(core * 256 + 128 * p, 128), 128) for p in range(2)]
    own_weights = (up_in, down_in)
    weights = (up, down)

    def weight_copy(which, hop):
        return pltpu.make_async_remote_copy(
            src_ref=own_weights[which].at[half],
            dst_ref=weights[which].at[hop, half],
            send_sem=w_send.at[which, hop // 2],
            recv_sem=w_recv.at[which, hop // 2],
            device_id=(s, (g + n_grp - hop) % n_grp),
            device_id_type=MESH,
        )

    def pass_copy(which, hop):
        at = part_rows[hop // 2]
        return pltpu.make_async_remote_copy(
            src_ref=weights[which].at[hop, at],
            dst_ref=weights[which].at[2, at],
            send_sem=t_send.at[which, hop // 2],
            recv_sem=t_recv.at[which, hop // 2],
            device_id=(s, (g + n_grp - hop % 2 + (hop // 2) * 2) % n_grp),
            device_id_type=MESH,
        )

    def twin_copy(which, hop):
        return pltpu.make_async_remote_copy(
            src_ref=weights[which].at[hop, half],
            dst_ref=weights[which].at[hop, half],
            send_sem=f_send.at[which, hop - 1],
            recv_sem=f_recv.at[which, hop - 1],
            device_id=(sibling, g),
            device_id_type=MESH,
        )

    def weights_on(which):
        for hop in (1, 3):
            weight_copy(which, hop).wait_recv()
            pass_copy(which, hop).start()
        for hop in (1, 3):
            twin_copy(which, hop).start()

    def weights_last(which):
        for hop in (1, 3):
            pass_copy(which, hop).wait_recv()
        twin_copy(which, 2).start()

    project(0)
    pl.semaphore_wait(barrier, n_grp - 1 + 2 + 7 + depth - 1)
    for index in range(3):
        halo_copy(0, index).start()
    for which in range(2):
        for hop in (1, 3):
            weight_copy(which, hop).start()
    for block in range(1, 4):
        project(block)
        for index in range(3):
            halo_copy(block, index).start()

    for k in range(1, 8):
        greet(late_sem, z * 8 + (yc + k) % 8, g)

    def halo_on(chunk):
        halo_copy(chunk, 0).wait_recv()
        halo_copy(chunk, 1).wait_recv()
        halo_copy(chunk, 3).start()

    factors = [scale[head] * (LOG2E / 64.0) for head in range(2)]

    top_rows = lax.broadcasted_iota(jnp.int32, (128, 1), 0) < 64

    def gathered(pieces):
        keys = jnp.concatenate([kv[chunk][slot, 0] for chunk, slot in pieces], axis=0)
        turned = []
        for chunk, slot in pieces:
            both = kv[chunk][slot, 1]
            turned += [both[:128], both[128:]]
        return keys, jnp.concatenate(turned, axis=1)

    def weighted(head, exponent, turned):
        values = jnp.where(top_rows == (head == 0), turned, jnp.asarray(1.0, BF16))
        return jnp.dot(values, exponent.astype(BF16), preferred_element_type=F32)

    def own_patch(head):
        keys, turned = gathered([(chunk, 2) for chunk in range(4)])
        for block in range(2):
            at = pl.ds(512 * block, 512)
            scores = jnp.dot(keys, queries[head, :, at], preferred_element_type=F32)
            top = jnp.max(scores, axis=0, keepdims=True)
            acc[head, :, at] = weighted(head, jnp.exp2((scores - top) * factors[head]), turned)
            tops[head, :, at] = top

    rels = [jnp.clip(patches[0, i] - s + 2, 0, 4) for i in (1, 2)]

    def added(chunk, head, at):
        keys, turned = gathered([(chunk, rel) for rel in rels])
        scores = jnp.dot(keys, queries[head, :, at], preferred_element_type=F32)
        own_top = tops[head, :, at]
        top = jnp.maximum(jnp.max(scores, axis=0, keepdims=True), own_top)
        total = acc[head, :, at] * jnp.exp2((own_top - top) * factors[head])
        return total + weighted(head, jnp.exp2((scores - top) * factors[head]), turned), top

    def halo_in(chunk):
        halo_copy(chunk, 2).wait_recv()
        halo_copy(chunk, 3).wait_recv()

    def stage(chunk):
        halo_in(chunk)
        at = pl.ds(0, PATCH)
        for head in range(2):
            total, top = added(chunk, head, at)
            acc[head, :, at] = total
            tops[head, :, at] = top

    own_patch(0)
    halo_on(0)
    own_patch(1)
    halo_on(1)
    weights_on(0)

    dest = dest_ref[...]
    dz = (dest // 8 - z + depth) % depth
    lag = jnp.minimum(dz, depth - dz)
    order = 2 * (depth // 2 - lag) - jnp.where(dz * 2 < depth, 0, 1)
    order = jnp.where(dz * 2 == depth, 0, jnp.where(dz == 0, depth - 1, order))
    position = order * 8 + (dest % 8 - yc + 8) % 8
    onehot = (lax.broadcasted_iota(jnp.int32, (n_seq, PATCH), 0) == position).astype(F32)
    earlier = (
        lax.broadcasted_iota(jnp.int32, (PATCH, PATCH), 0)
        < lax.broadcasted_iota(jnp.int32, (PATCH, PATCH), 1)
    ).astype(F32).astype(BF16)
    before = jnp.dot(onehot.astype(BF16), earlier, preferred_element_type=F32)
    rank = jnp.sum(before * onehot, axis=0, keepdims=True).astype(jnp.int32)
    slot = position * 16 + rank

    def place_rows(block, _):
        index = lax.broadcasted_iota(jnp.int32, (256, PATCH), 0) + block * 256
        place[block_of(block), :] = (index == slot).astype(F32).astype(BF16)
        return 0

    lax.fori_loop(0, n_seq * 16 // 256, place_rows, 0)

    stage(0)
    halo_on(2)
    stage(1)
    stage(2)
    halo_on(3)
    weights_on(1)
    halo_in(3)

    quarter = block_of(g, 128)

    def att_copy(turn):
        block = (g + 1 + turn) % n_grp
        return pltpu.make_async_remote_copy(
            src_ref=part.at[block_of(block)],
            dst_ref=att.at[:, quarter],
            send_sem=a_send.at[turn],
            recv_sem=a_recv.at[turn],
            device_id=(s, block),
            device_id_type=MESH,
        )

    def finish(block):
        at = block_of(block)
        first, _ = added(3, 0, at)
        second, _ = added(3, 1, at)
        joined = jnp.concatenate(
            [first[:64] / first[64:65], second[64:] / second[0:1]], axis=0
        )
        return joined.T.astype(BF16)

    def last_stage(turn, _):
        block = (g + 1 + turn) % n_grp
        part[block_of(block), :] = finish(block)
        att_copy(turn).start()
        return 0

    lax.fori_loop(0, 3, last_stage, 0)
    att[:, quarter] = finish(g)
    weights_last(0)

    mine = block_of(g)
    out_load.wait()
    up_load.wait()
    down_load.wait()
    for turn in range(3):
        att_copy(turn).wait_recv()
    resid = (
        tokens[mine, :].astype(F32)
        + jnp.dot(att[...], w_out[...], preferred_element_type=F32)
    ).astype(BF16)
    resid_wide = resid.astype(F32)
    normed = layer_norm(resid_wide).astype(BF16)

    def mlp(hop):
        hidden = gelu(jnp.dot(normed, up[hop], preferred_element_type=F32)).astype(BF16)
        product = jnp.dot(hidden, down[hop], preferred_element_type=F32)
        return product.astype(BF16).astype(F32)

    total = mlp(0)
    weights_last(1)
    for hop in (1, 3, 2):
        twin_copy(0, hop).wait_recv()
        twin_copy(1, hop).wait_recv()
        total = total + mlp(hop)
    rows_full[...] = (resid_wide + total).astype(BF16)

    def back_copy(hop):
        target = (g + hop) % n_grp
        return pltpu.make_async_remote_copy(
            src_ref=rows_full.at[:, block_of(target, 128)],
            dst_ref=rows.at[mine],
            send_sem=b_send.at[hop - 1],
            recv_sem=b_recv.at[hop - 1],
            device_id=(s, target),
            device_id_type=MESH,
        )

    for hop in (1, 3, 2):
        back_copy(hop).start()
    rows[mine, :] = rows_full[:, quarter]
    for hop in (1, 3, 2):
        back_copy(hop).wait_recv()

    pl.semaphore_wait(late_sem, 7)

    def relay_copy(k):
        m = k // 8
        h = (m + 1) // 2
        far = jnp.where(m % 2 == 1, depth // 2 + h, depth // 2 - h) % depth
        target = ((z + far) % depth) * 8 + (yc + k % 8) % 8
        return pltpu.make_async_remote_copy(
            src_ref=send_rows.at[block_of(k, 16)],
            dst_ref=out.at[block_of(s, 16)],
            send_sem=relay_send,
            recv_sem=relay_recv,
            device_id=(target, g),
            device_id_type=MESH,
        )

    def spread(chunk):
        at = block_of(chunk)
        send_rows[at, :] = jnp.dot(place[at, :], rows[...], preferred_element_type=F32).astype(BF16)

    def relay(k, _):
        relay_copy(k).start()
        return 0

    def relay_chunk(chunk, _):
        spread(chunk)
        lax.fori_loop(chunk * 16, chunk * 16 + 16, relay, 0)
        return 0

    last = n_seq // 16 - 1
    self_k = n_seq - 8
    lax.fori_loop(0, last, relay_chunk, 0)
    spread(last)
    lax.fori_loop(last * 16, self_k, relay, 0)
    lax.fori_loop(self_k + 1, n_seq, relay, 0)
    own = pltpu.make_async_copy(
        send_rows.at[pl.ds(self_k * 16, 16)], out.at[block_of(s, 16)], local_sem
    )
    own.start()
    own.wait()

    for which in range(2):
        for hop in (1, 3):
            weight_copy(which, hop).wait_send()
            pass_copy(which, hop).wait_send()
        for hop in (1, 2, 3):
            twin_copy(which, hop).wait_send()
    for chunk in range(4):
        for index in range(4):
            halo_copy(chunk, index).wait_send()
    for turn in range(3):
        att_copy(turn).wait_send()
        back_copy(turn + 1).wait_send()
    sent = pl.ds(0, (n_seq - 1) * 16)
    pltpu.make_async_copy(send_rows.at[sent], send_rows.at[sent], relay_send).wait()
    pltpu.make_async_copy(send_rows.at[sent], out.at[sent], relay_recv).wait()


def solution(mesh):
    n_seq = mesh.shape["seq"]
    n_grp = mesh.shape["grp"]

    def body(tokens, w_qkv, w_out, w_up, w_down, score_scale, patch_list, relay_dest):
        vmem = pl.BlockSpec(memory_space=pltpu.VMEM)
        hbm = pl.BlockSpec(memory_space=pl.ANY)
        smem = pl.BlockSpec(memory_space=pltpu.SMEM)
        dma = pltpu.SemaphoreType.DMA
        return pl.pallas_call(
            functools.partial(kernel, n_seq, n_grp),
            out_shape=jax.ShapeDtypeStruct((n_seq * 16, 128), BF16),
            in_specs=[hbm] * 5 + [smem, smem, vmem],
            out_specs=vmem,
            scratch_shapes=[
                pltpu.VMEM((PATCH, 512), BF16),
                pltpu.VMEM((3, 512, 128), BF16),
                pltpu.VMEM((512, 512), BF16),
                pltpu.VMEM((4, 512, 512), BF16),
                pltpu.VMEM((4, 512, 512), BF16),
                pltpu.VMEM((2, 128, PATCH), BF16),
                pltpu.VMEM((5, 2, 256, 128), BF16),
                pltpu.VMEM((5, 2, 256, 128), BF16),
                pltpu.VMEM((5, 2, 256, 128), BF16),
                pltpu.VMEM((5, 2, 256, 128), BF16),
                pltpu.VMEM((2, 128, PATCH), F32),
                pltpu.VMEM((2, 1, PATCH), F32),
                pltpu.VMEM((PATCH, 128), BF16),
                pltpu.VMEM((256, 512), BF16),
                pltpu.VMEM((256, 512), BF16),
                pltpu.VMEM((PATCH, 128), BF16),
                pltpu.VMEM((n_seq * 16, PATCH), BF16),
                pltpu.VMEM((n_seq * 16, 128), BF16),
                dma((8,)),
                dma((4, 4)),
                dma((4, 4)),
                dma((2, 2)),
                dma((2, 2)),
                dma((2, 2)),
                dma((2, 2)),
                dma((2, 3)),
                dma((2, 3)),
                dma((3,)),
                dma((3,)),
                dma((3,)),
                dma((3,)),
                dma,
                dma,
                dma,
                pltpu.SemaphoreType.REGULAR,
            ],
            compiler_params=pltpu.CompilerParams(
                collective_id=0, has_side_effects=True, vmem_limit_bytes=60 << 20
            ),
            name="block",
        )(tokens, w_qkv, w_out, w_up, w_down, score_scale, patch_list, relay_dest.reshape(1, PATCH))

    return jax.shard_map(
        body,
        mesh=mesh,
        in_specs=(
            P("seq", None),
            P(None, None, "grp"),
            P(),
            P(None, "grp"),
            P("grp", None),
            P("grp"),
            P("seq", None),
            P("seq", None),
        ),
        out_specs=P("seq", "grp"),
        check_vma=False,
    )
```

time: 86.5 us -> 80.4 us (0.929)
  Pallas kernels: 84.4 us -> 78.3 us
    pallas_call x1, Pallas kernels: 84.4 us -> 78.3 us  [body(): pl.pallas_call(functools.partial(kernel, n_seq, n_grp), out_shape=jax.Sha...]
where the time goes in v2:
time: 80.4 us; the launch traced here: 80.2 us
  Pallas kernels  78.3 us (97%)
  local copies, waits for them, and re-layouts  1.87 us (2%)
    pallas_call x1, Pallas kernels, body(): pl.pallas_call(functools.partial(kernel, n_seq, n_grp), out_shape=jax.Sha...  78.3 us
    unnamed x1, local copies, waits for them, and re-layouts  1.87 us

profile of v2, /device:TPU:1, one launch (start us, length us, event | category | flops | bytes accessed | tf_op | source)
XLA Modules:
  0.0 80.2 jit_solution(949785697306765055)
XLA Ops:
  0.0 78.3 %block.1 = bf16[2048,128]{1,0:T(8,128)(2,1)} custom-call(bf16[1024,512]{1,0:T(8,128)(2,1)} %tokens_in.1, bf16[3,512,128]{2,1,0:T(8,128)(2,1)} %qkv_in.1, bf16[512,512]{1,0:T(8,128)(2,1)} %out_in.1, bf16[512,512]{1,0:T(8,128)(2,1)} %up_in.1, bf16[512,512]{1,0:T(8,128)(2,1)} %down_in.1, f32[2]{0:T(128)} %scale.1, s32[1,3]{1,0:T(1,128)} %patches.1, ...), custom_call_target="tpu_custom_call" | custom-call | tf_op jit(solution)/shard_map/block/pallas_call | solution.py:417
  78.3 1.9 %copy.10 = bf16[2048,128]{1,0:T(8,128)(2,1)} copy(bf16[2048,128]{1,0:T(8,128)(2,1)} %block.1) | data formatting | bytes 1048576

commit v3 on v2

--- a/solution.py
+++ b/solution.py
@@ -43,7 +43,7 @@
     tokens, w_qkv, w_out, up, down, queries, kv_0, kv_1, kv_2, kv_3, acc, tops, part, att,
     rows_full, rows, place, send_rows,
     load_sem, halo_send, halo_recv, w_send, w_recv, t_send, t_recv, f_send, f_recv,
-    a_send, a_recv, b_send, b_recv, relay_send, relay_recv, local_sem, late_sem,
+    a_send, a_recv, b_send, b_recv, relay_send, relay_recv, local_sem, late_sem, ring_sem,
 ):
     s = lax.axis_index("seq")
     g = lax.axis_index("grp")
@@ -77,6 +77,9 @@
 
     barrier = pltpu.get_barrier_semaphore()
 
+    def along(hop):
+        return ((z + hop + depth) % depth) * 8 + yc
+
     def greet(sem, seq, grp):
         pl.semaphore_signal(sem, inc=1, device_id=(seq, grp), device_id_type=MESH)
 
@@ -86,8 +89,8 @@
         greet(barrier, (s + offset + n_seq) % n_seq, g)
     for k in range(1, 8):
         greet(barrier, z * 8 + (yc + k) % 8, g)
-    for k in range(1, depth):
-        greet(barrier, ((z + k) % depth) * 8 + yc, g)
+    for hop in (1, -1):
+        greet(barrier, along(hop), g)
 
     low = lax.broadcasted_iota(jnp.int32, (1, 128), 1) < 64
 
@@ -170,7 +173,16 @@
         twin_copy(which, 2).start()
 
     project(0)
-    pl.semaphore_wait(barrier, n_grp - 1 + 2 + 7 + depth - 1)
+    pl.semaphore_wait(barrier, n_grp - 1 + 2 + 7 + 2)
+
+    def ring_signal(step):
+        for hop in (1 << step, -(1 << step)):
+            greet(ring_sem.at[step], along(hop), g)
+
+    def ring_wait(step):
+        pl.semaphore_wait(ring_sem.at[step], 2)
+
+    ring_signal(0)
     for index in range(3):
         halo_copy(0, index).start()
     for which in range(2):
@@ -181,9 +193,6 @@
         for index in range(3):
             halo_copy(block, index).start()
 
-    for k in range(1, 8):
-        greet(late_sem, z * 8 + (yc + k) % 8, g)
-
     def halo_on(chunk):
         halo_copy(chunk, 0).wait_recv()
         halo_copy(chunk, 1).wait_recv()
@@ -238,6 +247,8 @@
 
     own_patch(0)
     halo_on(0)
+    ring_wait(0)
+    ring_signal(1)
     own_patch(1)
     halo_on(1)
     weights_on(0)
@@ -265,6 +276,8 @@
     lax.fori_loop(0, n_seq * 16 // 256, place_rows, 0)
 
     stage(0)
+    ring_wait(1)
+    ring_signal(2)
     halo_on(2)
     stage(1)
     stage(2)
@@ -285,23 +298,25 @@
             device_id_type=MESH,
         )
 
-    def finish(block):
-        at = block_of(block)
+    def finish(pair):
+        at = block_of(pair, 512)
         first, _ = added(3, 0, at)
         second, _ = added(3, 1, at)
         joined = jnp.concatenate(
             [first[:64] / first[64:65], second[64:] / second[0:1]], axis=0
         )
-        return joined.T.astype(BF16)
-
-    def last_stage(turn, _):
-        block = (g + 1 + turn) % n_grp
-        part[block_of(block), :] = finish(block)
-        att_copy(turn).start()
-        return 0
-
-    lax.fori_loop(0, 3, last_stage, 0)
-    att[:, quarter] = finish(g)
+        part[at, :] = joined.T.astype(BF16)
+
+    pair = 1 - g // 2
+    finish(pair)
+    for block in (2 * pair, 2 * pair + 1):
+        att_copy((block - g + 3) % n_grp).start()
+    finish(g // 2)
+    att_copy((g + 1 - 2 * (g % 2) - g + 3) % n_grp).start()
+    att[:, quarter] = part[block_of(g), :]
+    ring_wait(2)
+    for k in range(1, 8):
+        greet(late_sem, z * 8 + (yc + k) % 8, g)
     weights_last(0)
 
     mine = block_of(g)
@@ -455,6 +470,7 @@
                 dma,
                 dma,
                 pltpu.SemaphoreType.REGULAR,
+                pltpu.SemaphoreType.REGULAR((3,)),
             ],
             compiler_params=pltpu.CompilerParams(
                 collective_id=0, has_side_effects=True, vmem_limit_bytes=60 << 20

time: 80.4 us -> 77.1 us (0.959)
  Pallas kernels: 78.3 us -> 75 us
    pallas_call x1, Pallas kernels: 78.3 us -> 75 us  [body(): pl.pallas_call(functools.partial(kernel, n_seq, n_grp), out_shape=jax.Sha...]
where the time goes in v3:
time: 77.1 us; the launch traced here: 76.9 us
  Pallas kernels  75 us (97%)
  local copies, waits for them, and re-layouts  1.87 us (2%)
    pallas_call x1, Pallas kernels, body(): pl.pallas_call(functools.partial(kernel, n_seq, n_grp), out_shape=jax.Sha...  75 us
    unnamed x1, local copies, waits for them, and re-layouts  1.87 us

profile of v3, /device:TPU:1, one launch (start us, length us, event | category | flops | bytes accessed | tf_op | source)
XLA Modules:
  0.0 76.9 jit_solution(7008159032957844341)
XLA Ops:
  0.0 75.0 %block.1 = bf16[2048,128]{1,0:T(8,128)(2,1)} custom-call(bf16[1024,512]{1,0:T(8,128)(2,1)} %tokens_in.1, bf16[3,512,128]{2,1,0:T(8,128)(2,1)} %qkv_in.1, bf16[512,512]{1,0:T(8,128)(2,1)} %out_in.1, bf16[512,512]{1,0:T(8,128)(2,1)} %up_in.1, bf16[512,512]{1,0:T(8,128)(2,1)} %down_in.1, f32[2]{0:T(128)} %scale.1, s32[1,3]{1,0:T(1,128)} %patches.1, ...), custom_call_target="tpu_custom_call" | custom-call | tf_op jit(solution)/shard_map/block/pallas_call | solution.py:432
  75.0 1.9 %copy.10 = bf16[2048,128]{1,0:T(8,128)(2,1)} copy(bf16[2048,128]{1,0:T(8,128)(2,1)} %block.1) | data formatting | bytes 1048576

commit v4 on v3

--- a/solution.py
+++ b/solution.py
@@ -172,7 +172,6 @@
             pass_copy(which, hop).wait_recv()
         twin_copy(which, 2).start()
 
-    project(0)
     pl.semaphore_wait(barrier, n_grp - 1 + 2 + 7 + 2)
 
     def ring_signal(step):
@@ -183,11 +182,12 @@
         pl.semaphore_wait(ring_sem.at[step], 2)
 
     ring_signal(0)
-    for index in range(3):
-        halo_copy(0, index).start()
     for which in range(2):
         for hop in (1, 3):
             weight_copy(which, hop).start()
+    project(0)
+    for index in range(3):
+        halo_copy(0, index).start()
     for block in range(1, 4):
         project(block)
         for index in range(3):

time: 77.1 us -> 77.5 us (level)
  no operation moved by 1% of the time
where the time goes in v4:
time: 77.5 us; the launch traced here: 77.3 us
  Pallas kernels  75.5 us (97%)
  local copies, waits for them, and re-layouts  1.87 us (2%)
    pallas_call x1, Pallas kernels, body(): pl.pallas_call(functools.partial(kernel, n_seq, n_grp), out_shape=jax.Sha...  75.5 us
    unnamed x1, local copies, waits for them, and re-layouts  1.87 us

profile of v4, /device:TPU:1, one launch (start us, length us, event | category | flops | bytes accessed | tf_op | source)
XLA Modules:
  0.0 77.3 jit_solution(13763144173536014120)
XLA Ops:
  0.0 75.5 %block.1 = bf16[2048,128]{1,0:T(8,128)(2,1)} custom-call(bf16[1024,512]{1,0:T(8,128)(2,1)} %tokens_in.1, bf16[3,512,128]{2,1,0:T(8,128)(2,1)} %qkv_in.1, bf16[512,512]{1,0:T(8,128)(2,1)} %out_in.1, bf16[512,512]{1,0:T(8,128)(2,1)} %up_in.1, bf16[512,512]{1,0:T(8,128)(2,1)} %down_in.1, f32[2]{0:T(128)} %scale.1, s32[1,3]{1,0:T(1,128)} %patches.1, ...), custom_call_target="tpu_custom_call" | custom-call | tf_op jit(solution)/shard_map/block/pallas_call | solution.py:432
  75.5 1.9 %copy.10 = bf16[2048,128]{1,0:T(8,128)(2,1)} copy(bf16[2048,128]{1,0:T(8,128)(2,1)} %block.1) | data formatting | bytes 1048576
